TPU v7x, 32 devices: a whole 2x2x4 slice. The times are simulated.
32 devices in a mesh: groups: 2 (over y), expert: 8 (over z, core), dp: 2 (over x).
Axes of the slice: x: 2, y: 2, z: 4, core: 2. Of those that a mesh axis runs over, the one named last changes fastest.
Arguments:
- tokens: bfloat16 [4096, 2048], P(('groups', 'expert', 'dp')), parts along dimension 0, may hold values from -6 to 6
- out_grads: bfloat16 [4096, 2048], P(('groups', 'expert', 'dp')), parts along dimension 0, may hold values from -3 to 3
- routes: int32 [4096, 8], P(('groups', 'expert', 'dp')), parts along dimension 0, may hold values from 0 to 15, all different within a row; in each aligned block of 128 rows (0 to 127, 128 to 255, ...) at most 72 rows name the same one
- gates: bfloat16 [4096, 8], P(('groups', 'expert', 'dp')), parts along dimension 0, may hold values from 0.049804688 to 0.5
- gate_weight: bfloat16 [16, 2048, 384], P('expert'), may hold values from -0.125 to 0.125
- up_weight: bfloat16 [16, 2048, 384], P('expert'), may hold values from -0.125 to 0.125
- down_weight: bfloat16 [16, 384, 2048], P('expert'), may hold values from -0.3125 to 0.3125
Outputs:
- input_grads: bfloat16 [4096, 2048], P(('groups', 'expert', 'dp')), parts along dimension 0
- gate_grads: bfloat16 [4096, 8], P(('groups', 'expert', 'dp')), parts along dimension 0
- gate_weight_grads: bfloat16 [32, 2048, 384], P(('groups', 'expert'), 'dp'), parts along dimension 0
- up_weight_grads: bfloat16 [32, 2048, 384], P(('groups', 'expert'), 'dp'), parts along dimension 0
- down_weight_grads: bfloat16 [32, 384, 2048], P(('groups', 'expert'), None, 'dp'), parts along dimension 0
There are 2 independent parts, one for each index of `groups`. A program takes and returns all parts, laid end to end along the dimension named above; an argument that names none is the same for every part. Nothing has to cross between parts.
Inputs may be any that keep to these rules, and one draw needn't show every extreme that they name: `routes`: each row names 8 different experts; among the rows of one device no expert is named more than 72 times, and in every draw some expert is named exactly 72 times by the rows of some device.
All inputs are finite; a program needn't handle non-finite values.
Results may differ from a plain program's by a relative error of at most 0.012.
Values may be sent and summed in bfloat16 or wider, within the bound.
A program may use at most 128 MiB of HBM per device.

v0:
```python
import jax
import jax.numpy as jnp
from jax import lax
from jax.sharding import PartitionSpec as P


def project_in(rows_x, gate_weight, up_weight):
    pre_gate = jnp.einsum("slcd,ldf->slcf", rows_x, gate_weight, preferred_element_type=jnp.float32)
    pre_up = jnp.einsum("slcd,ldf->slcf", rows_x, up_weight, preferred_element_type=jnp.float32)
    return (pre_gate, pre_up)


def per_device(tokens, out_grads, routes, gates, gate_weight, up_weight, down_weight):
    tok_rows, feature_width = tokens.shape
    top_count = routes.shape[1]
    local_experts = gate_weight.shape[0]
    group_count = lax.axis_size("expert")
    expert_count = local_experts * group_count
    capacity = min(
        tok_rows, max(2, (tok_rows * top_count * 9 + expert_count * 8 - 1) // (expert_count * 8))
    )
    flat_routes = routes.reshape(-1)
    onehot = (flat_routes[:, None] == jnp.arange(expert_count, dtype=jnp.int32)[None, :]).astype(
        jnp.int32
    )
    positions = jnp.sum((jnp.cumsum(onehot, axis=0) - 1) * onehot, axis=1)
    slot_index = flat_routes * capacity + positions
    sentinel = tok_rows * top_count
    slot_table = (
        jnp.full((expert_count * capacity,), sentinel, jnp.int32)
        .at[slot_index]
        .set(jnp.arange(sentinel, dtype=jnp.int32))
    )
    owners = slot_table // top_count
    padded_x = jnp.concatenate([tokens, jnp.zeros((1, feature_width), tokens.dtype)], axis=0)
    padded_dy = jnp.concatenate([out_grads, jnp.zeros((1, feature_width), out_grads.dtype)], axis=0)
    padded_gate = jnp.concatenate([gates.reshape(-1), jnp.zeros((1,), gates.dtype)], axis=0)
    shape_rows = (group_count, local_experts * capacity, feature_width)
    block_shape = (group_count, local_experts, capacity, feature_width)
    send_x = jnp.take(padded_x, owners, axis=0).reshape(shape_rows)
    send_dy = jnp.take(padded_dy, owners, axis=0).reshape(shape_rows)
    send_gate = jnp.take(padded_gate, slot_table).reshape(group_count, local_experts * capacity)
    recv_x, recv_dy, recv_gate = (
        lax.all_to_all(send_x, "expert", split_axis=0, concat_axis=0, tiled=True),
        lax.all_to_all(send_dy, "expert", split_axis=0, concat_axis=0, tiled=True),
        lax.all_to_all(send_gate, "expert", split_axis=0, concat_axis=0, tiled=True),
    )
    pre_gate, pre_up = project_in(recv_x.reshape(block_shape), gate_weight, up_weight)
    rows_x = recv_x.reshape(block_shape)
    rows_dy = recv_dy.reshape(block_shape)
    gate_col = recv_gate.reshape(group_count, local_experts, capacity, 1).astype(jnp.float32)
    sigmoid_gate = jax.nn.sigmoid(pre_gate)
    activated = pre_gate * sigmoid_gate
    hidden = activated * pre_up
    gated_hidden = (gate_col * hidden).astype(jnp.bfloat16)
    back_raw = jnp.einsum(
        "slcd,lfd->slcf", rows_dy, down_weight, preferred_element_type=jnp.float32
    )
    route_grad = jnp.sum(hidden * back_raw, axis=-1).astype(jnp.bfloat16)
    back = gate_col * back_raw
    grad_gate = (back * pre_up * sigmoid_gate * (1.0 + pre_gate * (1.0 - sigmoid_gate))).astype(
        jnp.bfloat16
    )
    grad_up = (back * activated).astype(jnp.bfloat16)
    down_part = jnp.einsum(
        "slcf,slcd->lfd", gated_hidden, rows_dy, preferred_element_type=jnp.float32
    ).astype(jnp.bfloat16)
    row_grads = (
        jnp.einsum("slcf,ldf->slcd", grad_gate, gate_weight, preferred_element_type=jnp.float32)
        + jnp.einsum("slcf,ldf->slcd", grad_up, up_weight, preferred_element_type=jnp.float32)
    ).astype(jnp.bfloat16)
    back_rows, back_route = (
        lax.all_to_all(
            row_grads.reshape(shape_rows), "expert", split_axis=0, concat_axis=0, tiled=True
        ),
        lax.all_to_all(
            route_grad.reshape(group_count, local_experts * capacity),
            "expert",
            split_axis=0,
            concat_axis=0,
            tiled=True,
        ),
    )
    picked = jnp.take(back_rows.reshape(expert_count * capacity, feature_width), slot_index, axis=0)
    picked = picked.reshape(tok_rows, top_count, feature_width)
    input_grads = jnp.sum(picked, axis=1, dtype=jnp.float32).astype(jnp.bfloat16)
    gate_grads = jnp.take(back_route.reshape(-1), slot_index).reshape(tok_rows, top_count)
    gate_part = jnp.einsum(
        "slcd,slcf->ldf", rows_x, grad_gate, preferred_element_type=jnp.float32
    ).astype(jnp.bfloat16)
    up_part = jnp.einsum(
        "slcd,slcf->ldf", rows_x, grad_up, preferred_element_type=jnp.float32
    ).astype(jnp.bfloat16)
    gate_sum, up_sum, down_sum = (
        lax.psum_scatter(gate_part, "dp", scatter_dimension=1, tiled=True).astype(jnp.float32),
        lax.psum_scatter(up_part, "dp", scatter_dimension=1, tiled=True).astype(jnp.float32),
        lax.psum_scatter(down_part, "dp", scatter_dimension=2, tiled=True).astype(jnp.float32),
    )
    return (
        input_grads,
        gate_grads,
        gate_sum.astype(jnp.bfloat16),
        up_sum.astype(jnp.bfloat16),
        down_sum.astype(jnp.bfloat16),
    )


def solution(mesh):
    in_specs = (
        P(("groups", "expert", "dp"), None),
        P(("groups", "expert", "dp"), None),
        P(("groups", "expert", "dp"), None),
        P(("groups", "expert", "dp"), None),
        P("expert", None, None),
        P("expert", None, None),
        P("expert", None, None),
    )
    out_specs = (
        P(("groups", "expert", "dp"), None),
        P(("groups", "expert", "dp"), None),
        P(("groups", "expert"), "dp", None),
        P(("groups", "expert"), "dp", None),
        P(("groups", "expert"), None, "dp"),
    )
    return jax.shard_map(
        per_device, mesh=mesh, in_specs=in_specs, out_specs=out_specs, check_vma=False
    )
```

profile of v0, /device:TPU:0, one launch (start us, length us, event | category | flops | bytes accessed | tf_op | source)
XLA Modules:
  0.0 462.9 jit_solution(1576886883880407843)
XLA Ops:
  9.2 4.5 reduce-window.6
  14.3 4.3 scatter_custom_fusion
  18.7 7.3 %gather_fusion = bf16[1152]{0:T(1024)(128)(2,1)S(1)} fusion(bf16[1025]{0:T(1024)(128)(2,1)S(1)} %pad_maximum_fusion, s32[2048]{0:T(1024)S(1)} %pad_clamp_fusion.1), kind=kCustom, calls=%fused_computation.2 | custom fusion | bytes 9216 | tf_op jit(solution)/shard_map/jit(_take)/gather | solution.py:42
  26.7 6.3 %all-to-all-start = ((bf16[8,1,144]{2,1,0:T(2,128)(2,1)}), bf16[8,1,144]{2,1,0:T(2,128)(2,1)S(1)}, u32[]{:S(2)}, u32[]{:S(2)}) async-start(bf16[8,1,144]{2,1,0:T(2,128)(2,1)} %select_n.75), calls=%async_computation | async-start | bytes 16384 | tf_op jit(solution)/shard_map/all_to_all | solution.py:46
  36.8 11.9 %gather_fusion.3 = bf16[1152,2048]{1,0:T(8,128)(2,1)} fusion(bf16[129,2048]{1,0:T(8,128)(2,1)} %concatenate.10, s32[2048]{0:T(1024)S(1)} %pad_clamp_fusion), kind=kCustom, calls=%fused_computation.clone | custom fusion | bytes 9441792 | tf_op jit(solution)/shard_map/jit(_take)/gather | solution.py:41
  48.7 11.8 %gather_fusion.4 = bf16[1152,2048]{1,0:T(8,128)(2,1)} fusion(bf16[129,2048]{1,0:T(8,128)(2,1)} %concatenate.11, s32[2048]{0:T(1024)S(1)} %pad_clamp_fusion), kind=kCustom, calls=%fused_computation.1.clone | custom fusion | bytes 9441792 | tf_op jit(solution)/shard_map/jit(_take)/gather | solution.py:40
  60.5 8.7 %broadcast_select_fusion.1 = (bf16[1152,2048]{1,0:T(8,128)(2,1)}, bf16[1152,2048]{1,0:T(8,128)(2,1)}) fusion(bf16[1152,2048]{1,0:T(8,128)(2,1)} %gather_fusion.3, pred[1152]{0:T(1024)(128)(4,1)S(1)} %get-tuple-element.23, bf16[1152,2048]{1,0:T(8,128)(2,1)} %gather_fusion.4), kind=kLoop, calls=%fused_computation.12 | loop fusion | flops 4718592 | bytes 18875520 | tf_op jit(solution)/shard_map/jit(_take)/select_n | solution.py:41
  69.1 110.5 %all_to_all.27 = bf16[8,144,2048]{2,1,0:T(8,128)(2,1)} all-to-all(bf16[8,144,2048]{2,1,0:T(8,128)(2,1)} %bitcast.110), channel_id=1, replica_groups=mesh['groups'=2,'expert'=8,'dp'=2] {'expert'}, dimensions={0} | all-to-all | bytes 9437184 | tf_op jit(solution)/shard_map/all_to_all | solution.py:44
  179.7 4.6 all-to-all-start.1
  184.6 6.3 %fusion.2 = f32[2,8,72,384]{3,2,1,0:T(8,128)} fusion(bf16[8,2,72,2048]{3,2,1,0:T(8,128)(2,1)} %bitcast.112, bf16[2,2048,384]{2,1,0:T(8,128)(2,1)S(1)} %copy-done), kind=kOutput, calls=%fused_computation.15 | convolution fusion | flops 1811939328 | bytes 9633792 | tf_op jit(solution)/shard_map/slcd,ldf->slcf/dot_general | solution.py:8
  190.9 3.8 fusion.4
  194.8 94.7 %all-to-all-done.1 = bf16[8,144,2048]{2,1,0:T(8,128)(2,1)} async-done(((bf16[8,144,2048]{2,1,0:T(8,128)(2,1)}), bf16[8,144,2048]{2,1,0:T(8,128)(2,1)}, u32[]{:S(2)}, u32[]{:S(2)}) %all-to-all-start.1) | async-done | bytes 4718624 | tf_op jit(solution)/shard_map/all_to_all | solution.py:45
  289.5 7.9 %bitcast_convert_fusion = bf16[2,384,2048]{2,1,0:T(8,128)(2,1)} fusion(bf16[8,2,72,2048]{3,2,1,0:T(8,128)(2,1)} %bitcast.5, f32[8,2,72]{2,0,1:T(8,128)S(1)} %copy.53, f32[2,8,72,384]{3,2,1,0:T(8,128)} %fusion.4, f32[2,8,72,384]{3,2,1,0:T(8,128)} %fusion.2), kind=kOutput, calls=%fused_computation.7 | convolution fusion | flops 1816608768 | bytes 11407872 | tf_op jit(solution)/shard_map/slcf,slcd->lfd/dot_general | solution.py:65
  297.7 8.4 %fusion.25 = (bf16[8,2,72]{2,0,1:T(8,128)(2,1)S(1)}, bf16[8,2,72,384]{3,2,0,1:T(8,128)(2,1)}, bf16[8,2,72,384]{3,2,0,1:T(8,128)(2,1)S(1)}) fusion(f32[2,8,72,384]{3,2,1,0:T(8,128)} %fusion.4, f32[2,8,72,384]{3,2,1,0:T(8,128)} %fusion.2, f32[8,2,72]{2,0,1:T(8,128)S(1)} %copy.53, bf16[2,384,2048]{2,1,0:T(8,128)(2,1)} %param.15, ...), kind=kOutput, calls=%fused_computation.43 | convolution fusion | flops 1819458432 | bytes 13179648 | tf_op jit(solution)/shard_map/slcd,lfd->slcf/dot_general | solution.py:56
  307.0 7.2 %bitcast_convert_fusion.1 = bf16[2,2048,384]{2,1,0:T(8,128)(2,1)} fusion(bf16[8,2,72,2048]{3,2,1,0:T(8,128)(2,1)} %bitcast.113, bf16[8,2,72,384]{3,2,0,1:T(8,128)(2,1)S(1)} %get-tuple-element.27), kind=kOutput, calls=%fused_computation.8 | convolution fusion | flops 1813512192 | bytes 8749056 | tf_op jit(solution)/shard_map/slcd,slcf->ldf/dot_general | solution.py:91
  315.0 3.3 all-to-all-start.4
  318.3 4.0 fusion.12
  322.3 4.2 fusion
  329.1 5.0 %all-to-all-start.3 = ((bf16[8,144,2048]{2,1,0:T(8,128)(2,1)}), bf16[8,144,2048]{2,1,0:T(8,128)(2,1)}, u32[]{:S(2)}, u32[]{:S(2)}) async-start(bf16[8,144,2048]{2,1,0:T(8,128)(2,1)} %bitcast.111), calls=%async_computation.3 | async-start | bytes 9437184 | tf_op jit(solution)/shard_map/all_to_all | solution.py:73
  334.4 7.5 %bitcast_convert_fusion.2 = bf16[2,2048,384]{2,1,0:T(8,128)(2,1)} fusion(bf16[8,2,72,2048]{3,2,1,0:T(8,128)(2,1)} %bitcast.114, bf16[8,2,72,384]{3,2,0,1:T(8,128)(2,1)} %get-tuple-element.26), kind=kOutput, calls=%fused_computation.9 | convolution fusion | flops 1813512192 | bytes 8749056 | tf_op jit(solution)/shard_map/slcd,slcf->ldf/dot_general | solution.py:88
  342.1 6.8 %gather_fusion.2 = bf16[1024]{0:T(1024)(128)(2,1)S(1)} fusion(bf16[1152]{0:T(1024)(128)(2,1)S(1)} %reshape.172, s32[1024]{0:T(1024)S(1)} %broadcast_clamp_fusion), kind=kCustom, calls=%fused_computation.4 | custom fusion | bytes 8192 | tf_op jit(solution)/shard_map/jit(_take)/gather | solution.py:87
  349.7 89.7 %all-to-all-done.3 = bf16[8,144,2048]{2,1,0:T(8,128)(2,1)} async-done(((bf16[8,144,2048]{2,1,0:T(8,128)(2,1)}), bf16[8,144,2048]{2,1,0:T(8,128)(2,1)}, u32[]{:S(2)}, u32[]{:S(2)}) %all-to-all-start.3) | async-done | bytes 4718624 | tf_op jit(solution)/shard_map/all_to_all | solution.py:73
  439.5 11.8 %gather_fusion.1 = bf16[1024,2048]{1,0:T(8,128)(2,1)} fusion(bf16[1152,2048]{1,0:T(8,128)(2,1)} %bitcast.20, s32[1024]{0:T(1024)S(1)} %broadcast_clamp_fusion), kind=kCustom, calls=%fused_computation.3 | custom fusion | bytes 8392704 | tf_op jit(solution)/shard_map/jit(_take)/gather | solution.py:84
  451.2 5.1 %fusion.1 = bf16[128,2048]{1,0:T(8,128)(2,1)} fusion(bf16[1024,2048]{1,0:T(8,128)(2,1)} %gather_fusion.1, pred[128,8]{1,0:T(8,128)(4,1)S(1)} %get-tuple-element.22), kind=kLoop, calls=%fused_computation.14 | loop fusion | flops 3932160 | bytes 4719616 | tf_op jit(solution)/shard_map/reduce_sum | solution.py:86
  (60 shorter events, 13.3 us)
Async XLA Ops:
  7.2 177.5 %copy-start = (bf16[2,2048,384]{2,1,0:T(8,128)(2,1)S(1)}, bf16[2,2048,384]{2,1,0:T(8,128)(2,1)}, u32[]{:S(2)}) copy-start(bf16[2,2048,384]{2,1,0:T(8,128)(2,1)} %param.13) | copy-start | bytes 9437188
  26.7 42.5 %all-to-all-start = ((bf16[8,1,144]{2,1,0:T(2,128)(2,1)}), bf16[8,1,144]{2,1,0:T(2,128)(2,1)S(1)}, u32[]{:S(2)}, u32[]{:S(2)}) async-start(bf16[8,1,144]{2,1,0:T(2,128)(2,1)} %select_n.75), calls=%async_computation | async-start | bytes 16384 | tf_op jit(solution)/shard_map/all_to_all | solution.py:46
  179.7 109.9 %all-to-all-start.1 = ((bf16[8,144,2048]{2,1,0:T(8,128)(2,1)}), bf16[8,144,2048]{2,1,0:T(8,128)(2,1)}, u32[]{:S(2)}, u32[]{:S(2)}) async-start(bf16[8,144,2048]{2,1,0:T(8,128)(2,1)} %bitcast.109), calls=%async_computation.1 | async-start | bytes 9437184 | tf_op jit(solution)/shard_map/all_to_all | solution.py:45
  184.3 272.1 %reduce-scatter.8.cloned.1.call-start = ((), (), s32[]{:S(2)}) async-start(), calls=%async_computation.10 | async-start | bytes 4718592 | tf_op jit(solution)/shard_map/reduce_scatter | solution.py:97
  184.6 6.3 %copy-start.1 = (bf16[8,144,2048]{2,1,0:T(8,128)(2,1)S(1)}, bf16[8,144,2048]{2,1,0:T(8,128)(2,1)}, u32[]{:S(2)}) copy-start(bf16[8,144,2048]{2,1,0:T(8,128)(2,1)} %all_to_all.27) | copy-start | bytes 14155780
  184.6 6.3 %copy-start.2 = (bf16[2,2048,384]{2,1,0:T(8,128)(2,1)S(1)}, bf16[2,2048,384]{2,1,0:T(8,128)(2,1)}, u32[]{:S(2)}) copy-start(bf16[2,2048,384]{2,1,0:T(8,128)(2,1)} %param.14) | copy-start | bytes 9437188
  297.4 158.9 %reduce-scatter.6.cloned.1.call-start = ((), (), s32[]{:S(2)}) async-start(), calls=%async_computation.9 | async-start | bytes 4718592 | tf_op jit(solution)/shard_map/reduce_scatter | solution.py:96
  306.1 0.9 copy-start.4
  315.0 14.1 %all-to-all-start.4 = ((bf16[8,1,144]{2,1,0:T(2,128)(2,1)}), bf16[8,1,144]{2,1,0:T(2,128)(2,1)S(1)}, u32[]{:S(2)}, u32[]{:S(2)}) async-start(bf16[8,1,144]{2,1,0:T(2,128)(2,1)} %convert_element_type.76), calls=%async_computation.4 | async-start | bytes 16384 | tf_op jit(solution)/shard_map/all_to_all | solution.py:76
  318.3 4.0 copy-start.3
  329.1 110.4 %all-to-all-start.3 = ((bf16[8,144,2048]{2,1,0:T(8,128)(2,1)}), bf16[8,144,2048]{2,1,0:T(8,128)(2,1)}, u32[]{:S(2)}, u32[]{:S(2)}) async-start(bf16[8,144,2048]{2,1,0:T(8,128)(2,1)} %bitcast.111), calls=%async_computation.3 | async-start | bytes 9437184 | tf_op jit(solution)/shard_map/all_to_all | solution.py:73
  334.1 122.3 %reduce-scatter.4.cloned.1.call-start = ((), (), s32[]{:S(2)}) async-start(), calls=%async_computation.8 | async-start | bytes 4718592 | tf_op jit(solution)/shard_map/reduce_scatter | solution.py:95
Sparse Core Ops, SparseCore 0:
  297.5 42.2 reduce-scatter.7
  342.7 43.3 reduce-scatter.5
  388.9 43.3 reduce-scatter.3
where the time goes:
time: 464 us; the launch traced here: 463 us
  waiting for transfers between devices  184 us (40%)
  blocking collectives  111 us (24%)
  local copies, waits for them, and re-layouts  65.9 us (14%)
  matrix products  49.3 us (11%)
  starting transfers between devices  20.1 us (4%)
  other arithmetic  18.7 us (4%)
  between operations  14 us (3%)
    all_to_all x1, blocking collectives, per_device(): lax.all_to_all(send_x, 'expert', split_axis=0, concat_axis=0, tiled=True)  111 us
    all_to_all x1, waiting for transfers between devices, per_device(): lax.all_to_all(send_dy, 'expert', split_axis=0, concat_axis=0, tiled=True)  94.7 us
    all_to_all x1, waiting for transfers between devices, per_device(): lax.all_to_all(row_grads.reshape(shape_rows), 'expert', split_axis=0, con...  89.7 us
    gather x1, local copies, waits for them, and re-layouts, per_device(): send_dy = jnp.take(padded_dy, owners, axis=0).reshape(shape_rows)  11.9 us
    gather x1, local copies, waits for them, and re-layouts, per_device(): jnp.take(back_rows.reshape(expert_count * capacity, feature_width), slot_...  11.8 us
    gather x1, local copies, waits for them, and re-layouts, per_device(): send_x = jnp.take(padded_x, owners, axis=0).reshape(shape_rows)  11.8 us
  transfers between devices with their start and end apart: 7, of which 2 were waited for; matrix products, arithmetic and copies ran while one was open for 23% of the time, Pallas kernels for 0%

commit v1 on v0

--- a/solution.py
+++ b/solution.py
@@ -2,6 +2,28 @@
 import jax.numpy as jnp
 from jax import lax
 from jax.sharding import PartitionSpec as P
+
+
+def cut_along(array, dim, size):
+    before, after = (array.shape[:dim], array.shape[dim + 1 :])
+    return jnp.moveaxis(array.reshape(*before, size, -1, *after), dim, 0)
+
+
+def joined_along(tiles, dim):
+    shape = list(tiles.shape[1:])
+    shape[dim] *= tiles.shape[0]
+    return jnp.moveaxis(tiles, 0, dim).reshape(shape)
+
+
+def pairwise_exchange(shard, axis, split_dim, concat_dim):
+    peers, index = (lax.axis_size(axis), lax.axis_index(axis))
+    parts = cut_along(shard, split_dim, peers)
+    done = [parts[index]]
+    for step in range(1, peers):
+        sent = parts[index ^ step]
+        done.append(lax.ppermute(sent, axis, [(i, i ^ step) for i in range(peers)]))
+    parts = jnp.stack(done)[index ^ jnp.arange(peers)]
+    return joined_along(parts, concat_dim)
 
 
 def project_in(rows_x, gate_weight, up_weight):
@@ -70,9 +92,7 @@
         + jnp.einsum("slcf,ldf->slcd", grad_up, up_weight, preferred_element_type=jnp.float32)
     ).astype(jnp.bfloat16)
     back_rows, back_route = (
-        lax.all_to_all(
-            row_grads.reshape(shape_rows), "expert", split_axis=0, concat_axis=0, tiled=True
-        ),
+        pairwise_exchange(row_grads.reshape(shape_rows), "expert", 0, 0),
         lax.all_to_all(
             route_grad.reshape(group_count, local_experts * capacity),
             "expert",

time: 464 us -> 480 us (1.034)
  local copies, waits for them, and re-layouts: 65.9 us -> 83.1 us
  waiting for transfers between devices: 184 us -> 179 us
    all_to_all x1 -> x0, waiting for transfers between devices: 89.7 us -> none  [per_device(): lax.all_to_all(row_grads.reshape(shape_rows), 'expert', split_axis=0, con...]
    ppermute x0 -> x7, waiting for transfers between devices: none -> 83.8 us  [pairwise_exchange(): done.append(lax.ppermute(sent, axis, [(i, i ^ step) for i in range(peers)]))]
    unnamed x13 -> x19, local copies, waits for them, and re-layouts: 3.35 us -> 13.1 us
    ppermute x0 -> x7, starting transfers between devices: none -> 8.98 us  [pairwise_exchange(): done.append(lax.ppermute(sent, axis, [(i, i ^ step) for i in range(peers)]))]
    gather x0 -> x1, local copies, waits for them, and re-layouts: none -> 5.34 us  [pairwise_exchange(): parts = jnp.stack(done)[index ^ jnp.arange(peers)]]
    all_to_all x1 -> x0, starting transfers between devices: 5 us -> none  [per_device(): lax.all_to_all(row_grads.reshape(shape_rows), 'expert', split_axis=0, con...]
  transfers between devices with their start and end apart: 7 -> 13, of which waited for: 2 -> 4; matrix products, arithmetic and copies ran while one was open for 23% -> 26% of each run, Pallas kernels for 0% -> 0%
where the time goes in v1:
time: 480 us; the launch traced here: 479 us
  waiting for transfers between devices  179 us (37%)
  blocking collectives  111 us (23%)
  local copies, waits for them, and re-layouts  83.1 us (17%)
  matrix products  49.2 us (10%)
  starting transfers between devices  24.3 us (5%)
  other arithmetic  18.7 us (4%)
  between operations  14 us (3%)
    all_to_all x1, blocking collectives, per_device(): lax.all_to_all(send_x, 'expert', split_axis=0, concat_axis=0, tiled=True)  111 us
    all_to_all x1, waiting for transfers between devices, per_device(): lax.all_to_all(send_dy, 'expert', split_axis=0, concat_axis=0, tiled=True)  94.8 us
    ppermute x7, waiting for transfers between devices, pairwise_exchange(): done.append(lax.ppermute(sent, axis, [(i, i ^ step) for i in range(peers)]))  83.8 us
    unnamed x19, local copies, waits for them, and re-layouts  13.1 us
    gather x1, local copies, waits for them, and re-layouts, per_device(): send_dy = jnp.take(padded_dy, owners, axis=0).reshape(shape_rows)  11.8 us
    gather x1, local copies, waits for them, and re-layouts, per_device(): send_x = jnp.take(padded_x, owners, axis=0).reshape(shape_rows)  11.8 us
    gather x1, local copies, waits for them, and re-layouts, per_device(): jnp.take(back_rows.reshape(expert_count * capacity, feature_width), slot_...  11.8 us
  transfers between devices with their start and end apart: 13, of which 4 were waited for; matrix products, arithmetic and copies ran while one was open for 26% of the time, Pallas kernels for 0%

profile of v1, /device:TPU:0, one launch (start us, length us, event | category | flops | bytes accessed | tf_op | source)
XLA Modules:
  0.0 478.5 jit_solution(13823452807296623011)
XLA Ops:
  8.3 4.5 reduce-window.6
  13.4 4.3 scatter_custom_fusion
  18.7 7.3 %gather_fusion = bf16[1152]{0:T(1024)(128)(2,1)S(1)} fusion(bf16[1025]{0:T(1024)(128)(2,1)S(1)} %pad_maximum_fusion, s32[2048]{0:T(1024)S(1)} %get-tuple-element.39), kind=kCustom, calls=%fused_computation.2 | custom fusion | bytes 9216 | tf_op jit(solution)/shard_map/jit(_take)/gather | solution.py:64
  26.7 6.3 %all-to-all-start = ((bf16[8,1,144]{2,1,0:T(2,128)(2,1)}), bf16[8,1,144]{2,1,0:T(2,128)(2,1)S(1)}, u32[]{:S(2)}, u32[]{:S(2)}) async-start(bf16[8,1,144]{2,1,0:T(2,128)(2,1)} %select_n.118), calls=%async_computation | async-start | bytes 16384 | tf_op jit(solution)/shard_map/all_to_all | solution.py:68
  36.8 11.8 %gather_fusion.4 = bf16[1152,2048]{1,0:T(8,128)(2,1)} fusion(bf16[129,2048]{1,0:T(8,128)(2,1)} %concatenate.10, s32[2048]{0:T(1024)S(1)} %get-tuple-element.38), kind=kCustom, calls=%fused_computation.clone | custom fusion | bytes 9441792 | tf_op jit(solution)/shard_map/jit(_take)/gather | solution.py:63
  48.7 11.8 %gather_fusion.5 = bf16[1152,2048]{1,0:T(8,128)(2,1)} fusion(bf16[129,2048]{1,0:T(8,128)(2,1)} %concatenate.11, s32[2048]{0:T(1024)S(1)} %get-tuple-element.38), kind=kCustom, calls=%fused_computation.1.clone | custom fusion | bytes 9441792 | tf_op jit(solution)/shard_map/jit(_take)/gather | solution.py:62
  60.4 8.7 %broadcast_select_fusion.1 = (bf16[1152,2048]{1,0:T(8,128)(2,1)}, bf16[1152,2048]{1,0:T(8,128)(2,1)}) fusion(bf16[1152,2048]{1,0:T(8,128)(2,1)} %gather_fusion.4, pred[1152]{0:T(1024)(128)(4,1)S(1)} %get-tuple-element.23, bf16[1152,2048]{1,0:T(8,128)(2,1)} %gather_fusion.5), kind=kLoop, calls=%fused_computation.13 | loop fusion | flops 4718592 | bytes 18875520 | tf_op jit(solution)/shard_map/jit(_take)/select_n | solution.py:63
  69.1 110.5 %all_to_all.22 = bf16[8,144,2048]{2,1,0:T(8,128)(2,1)} all-to-all(bf16[8,144,2048]{2,1,0:T(8,128)(2,1)} %bitcast.142), channel_id=1, replica_groups=mesh['groups'=2,'expert'=8,'dp'=2] {'expert'}, dimensions={0} | all-to-all | bytes 9437184 | tf_op jit(solution)/shard_map/all_to_all | solution.py:66
  179.6 4.6 all-to-all-start.1
  184.6 6.3 %fusion.2 = f32[2,8,72,384]{3,2,1,0:T(8,128)} fusion(bf16[8,2,72,2048]{3,2,1,0:T(8,128)(2,1)} %bitcast.145, bf16[2,2048,384]{2,1,0:T(8,128)(2,1)S(1)} %copy-done), kind=kOutput, calls=%fused_computation.16 | convolution fusion | flops 1811939328 | bytes 9633792 | tf_op jit(solution)/shard_map/slcd,ldf->slcf/dot_general | solution.py:30
  194.7 94.8 %all-to-all-done.1 = bf16[8,144,2048]{2,1,0:T(8,128)(2,1)} async-done(((bf16[8,144,2048]{2,1,0:T(8,128)(2,1)}), bf16[8,144,2048]{2,1,0:T(8,128)(2,1)}, u32[]{:S(2)}, u32[]{:S(2)}) %all-to-all-start.1) | async-done | bytes 4718624 | tf_op jit(solution)/shard_map/all_to_all | solution.py:67
  289.5 7.9 %bitcast_convert_fusion = bf16[2,384,2048]{2,1,0:T(8,128)(2,1)} fusion(bf16[8,2,72,2048]{3,2,1,0:T(8,128)(2,1)} %bitcast.5, f32[8,2,72]{2,0,1:T(8,128)S(1)} %copy.53, f32[2,8,72,384]{3,2,1,0:T(8,128)} %fusion.4, f32[2,8,72,384]{3,2,1,0:T(8,128)} %fusion.2), kind=kOutput, calls=%fused_computation.8 | convolution fusion | flops 1816608768 | bytes 11407872 | tf_op jit(solution)/shard_map/slcf,slcd->lfd/dot_general | solution.py:87
  297.6 8.4 %fusion.25 = (bf16[8,2,72]{2,0,1:T(8,128)(2,1)S(1)}, bf16[8,2,72,384]{3,2,0,1:T(8,128)(2,1)}, bf16[8,2,72,384]{3,2,0,1:T(8,128)(2,1)S(1)}) fusion(f32[2,8,72,384]{3,2,1,0:T(8,128)} %fusion.4, f32[2,8,72,384]{3,2,1,0:T(8,128)} %fusion.2, f32[8,2,72]{2,0,1:T(8,128)S(1)} %copy.53, bf16[2,384,2048]{2,1,0:T(8,128)(2,1)} %param.15, ...), kind=kOutput, calls=%fused_computation.44 | convolution fusion | flops 1819458432 | bytes 13179648 | tf_op jit(solution)/shard_map/slcd,lfd->slcf/dot_general | solution.py:78
  307.0 7.2 %bitcast_convert_fusion.1 = bf16[2,2048,384]{2,1,0:T(8,128)(2,1)} fusion(bf16[8,2,72,2048]{3,2,1,0:T(8,128)(2,1)} %bitcast.146, bf16[8,2,72,384]{3,2,0,1:T(8,128)(2,1)S(1)} %get-tuple-element.35), kind=kOutput, calls=%fused_computation.9 | convolution fusion | flops 1813512192 | bytes 8749056 | tf_op jit(solution)/shard_map/slcd,slcf->ldf/dot_general | solution.py:111
  314.6 7.5 %bitcast_convert_fusion.2 = bf16[2,2048,384]{2,1,0:T(8,128)(2,1)} fusion(bf16[8,2,72,2048]{3,2,1,0:T(8,128)(2,1)} %bitcast.147, bf16[8,2,72,384]{3,2,0,1:T(8,128)(2,1)} %get-tuple-element.26), kind=kOutput, calls=%fused_computation.10 | convolution fusion | flops 1813512192 | bytes 8749056 | tf_op jit(solution)/shard_map/slcd,slcf->ldf/dot_general | solution.py:108
  322.1 4.0 fusion.12
  326.1 4.1 fusion
  345.0 6.8 %gather_fusion.3 = bf16[1024]{0:T(1024)(128)(2,1)S(1)} fusion(bf16[1152]{0:T(1024)(128)(2,1)S(1)} %reshape.180, s32[1024]{0:T(1024)S(1)} %broadcast_clamp_fusion), kind=kCustom, calls=%fused_computation.5 | custom fusion | bytes 8192 | tf_op jit(solution)/shard_map/jit(_take)/gather | solution.py:107
  354.6 38.2 %collective-permute-done.1 = bf16[1,144,2048]{2,1,0:T(8,128)(2,1)} collective-permute-done((bf16[1,144,2048]{2,1,0:T(8,128)(2,1)}, bf16[1,144,2048]{2,1,0:T(8,128)(2,1)}, u32[]{:S(2)}, u32[]{:S(2)}) %collective-permute-start.1) | collective-permute-done | bytes 589856 | tf_op jit(solution)/shard_map/ppermute | solution.py:24
  396.6 8.9 %collective-permute-done.2 = bf16[1,144,2048]{2,1,0:T(8,128)(2,1)S(1)} collective-permute-done((bf16[1,144,2048]{2,1,0:T(8,128)(2,1)}, bf16[1,144,2048]{2,1,0:T(8,128)(2,1)S(1)}, u32[]{:S(2)}, u32[]{:S(2)}) %collective-permute-start.2) | collective-permute-done | bytes 589856 | tf_op jit(solution)/shard_map/ppermute | solution.py:24
  406.4 36.7 %collective-permute-done.3 = bf16[1,144,2048]{2,1,0:T(8,128)(2,1)S(1)} collective-permute-done((bf16[1,144,2048]{2,1,0:T(8,128)(2,1)}, bf16[1,144,2048]{2,1,0:T(8,128)(2,1)S(1)}, u32[]{:S(2)}, u32[]{:S(2)}) %collective-permute-start.3) | collective-permute-done | bytes 589856 | tf_op jit(solution)/shard_map/ppermute | solution.py:24
  449.7 5.3 %gather_fusion.1 = bf16[8,144,2048]{2,1,0:T(8,128)(2,1)} fusion(bf16[8,144,2048]{2,1,0:T(8,128)(2,1)} %bitcast.144, s32[1024]{0:T(1024)S(1)} %pad_clamp_fusion.2), kind=kCustom, calls=%fused_computation.3 | custom fusion | bytes 9437216 | tf_op jit(solution)/shard_map/gather | solution.py:25
  455.1 11.8 %gather_fusion.2 = bf16[1024,2048]{1,0:T(8,128)(2,1)} fusion(bf16[1152,2048]{1,0:T(8,128)(2,1)} %bitcast.140, s32[1024]{0:T(1024)S(1)} %broadcast_clamp_fusion), kind=kCustom, calls=%fused_computation.4 | custom fusion | bytes 8392704 | tf_op jit(solution)/shard_map/jit(_take)/gather | solution.py:104
  466.8 5.1 %fusion.1 = bf16[128,2048]{1,0:T(8,128)(2,1)} fusion(bf16[1024,2048]{1,0:T(8,128)(2,1)} %gather_fusion.2, pred[128,8]{1,0:T(8,128)(4,1)S(1)} %get-tuple-element.22), kind=kLoop, calls=%fused_computation.15 | loop fusion | flops 3932160 | bytes 4719616 | tf_op jit(solution)/shard_map/reduce_sum | solution.py:106
  (82 shorter events, 41.6 us)
Async XLA Ops:
  7.2 177.4 %copy-start = (bf16[2,2048,384]{2,1,0:T(8,128)(2,1)S(1)}, bf16[2,2048,384]{2,1,0:T(8,128)(2,1)}, u32[]{:S(2)}) copy-start(bf16[2,2048,384]{2,1,0:T(8,128)(2,1)} %param.13) | copy-start | bytes 9437188
  26.7 42.4 %all-to-all-start = ((bf16[8,1,144]{2,1,0:T(2,128)(2,1)}), bf16[8,1,144]{2,1,0:T(2,128)(2,1)S(1)}, u32[]{:S(2)}, u32[]{:S(2)}) async-start(bf16[8,1,144]{2,1,0:T(2,128)(2,1)} %select_n.118), calls=%async_computation | async-start | bytes 16384 | tf_op jit(solution)/shard_map/all_to_all | solution.py:68
  179.6 109.9 %all-to-all-start.1 = ((bf16[8,144,2048]{2,1,0:T(8,128)(2,1)}), bf16[8,144,2048]{2,1,0:T(8,128)(2,1)}, u32[]{:S(2)}, u32[]{:S(2)}) async-start(bf16[8,144,2048]{2,1,0:T(8,128)(2,1)} %bitcast.141), calls=%async_computation.1 | async-start | bytes 9437184 | tf_op jit(solution)/shard_map/all_to_all | solution.py:67
  184.2 287.8 %reduce-scatter.8.cloned.1.call-start = ((), (), s32[]{:S(2)}) async-start(), calls=%async_computation.9 | async-start | bytes 4718592 | tf_op jit(solution)/shard_map/reduce_scatter | solution.py:117
  184.6 6.3 %copy-start.1 = (bf16[8,144,2048]{2,1,0:T(8,128)(2,1)S(1)}, bf16[8,144,2048]{2,1,0:T(8,128)(2,1)}, u32[]{:S(2)}) copy-start(bf16[8,144,2048]{2,1,0:T(8,128)(2,1)} %all_to_all.22) | copy-start | bytes 14155780
  184.6 6.3 %copy-start.2 = (bf16[2,2048,384]{2,1,0:T(8,128)(2,1)S(1)}, bf16[2,2048,384]{2,1,0:T(8,128)(2,1)}, u32[]{:S(2)}) copy-start(bf16[2,2048,384]{2,1,0:T(8,128)(2,1)} %param.14) | copy-start | bytes 9437188
  297.4 174.6 %reduce-scatter.6.cloned.1.call-start = ((), (), s32[]{:S(2)}) async-start(), calls=%async_computation.8 | async-start | bytes 4718592 | tf_op jit(solution)/shard_map/reduce_scatter | solution.py:116
  306.1 0.9 copy-start.4
  314.2 157.8 %reduce-scatter.4.cloned.1.call-start = ((), (), s32[]{:S(2)}) async-start(), calls=%async_computation.7 | async-start | bytes 4718592 | tf_op jit(solution)/shard_map/reduce_scatter | solution.py:115
  322.1 4.0 copy-start.3
  333.1 19.5 %collective-permute-start = (bf16[1,144,2048]{2,1,0:T(8,128)(2,1)}, bf16[1,144,2048]{2,1,0:T(8,128)(2,1)}, u32[]{:S(2)}, u32[]{:S(2)}) collective-permute-start(bf16[1,144,2048]{2,1,0:T(8,128)(2,1)} %get-tuple-element.33), channel_id=1, source_target_pairs={{0,2},{2,0},{4,6},{6,4},{8,10},{10,8},{12,14},{14,12},{1,3},{3,1},... | collective-permute-start | bytes 1769480 | tf_op jit(solution)/shard_map/ppermute | solution.py:24
  333.8 11.1 %all-to-all-start.3 = ((bf16[8,1,144]{2,1,0:T(2,128)(2,1)}), bf16[8,1,144]{2,1,0:T(2,128)(2,1)S(1)}, u32[]{:S(2)}, u32[]{:S(2)}) async-start(bf16[8,1,144]{2,1,0:T(2,128)(2,1)} %convert_element_type.76), calls=%async_computation.3 | async-start | bytes 16384 | tf_op jit(solution)/shard_map/all_to_all | solution.py:96
  337.5 110.3 %collective-permute-start.6 = (bf16[1,144,2048]{2,1,0:T(8,128)(2,1)}, bf16[1,144,2048]{2,1,0:T(8,128)(2,1)}, u32[]{:S(2)}, u32[]{:S(2)}) collective-permute-start(bf16[1,144,2048]{2,1,0:T(8,128)(2,1)} %get-tuple-element.27), channel_id=1, source_target_pairs={{0,14},{2,12},{4,10},{6,8},{8,6},{10,4},{12,2},{14,0},{1,15},{3,13... | collective-permute-start | bytes 1769480 | tf_op jit(solution)/shard_map/ppermute | solution.py:24
  340.8 105.1 %collective-permute-start.5 = (bf16[1,144,2048]{2,1,0:T(8,128)(2,1)}, bf16[1,144,2048]{2,1,0:T(8,128)(2,1)}, u32[]{:S(2)}, u32[]{:S(2)}) collective-permute-start(bf16[1,144,2048]{2,1,0:T(8,128)(2,1)} %get-tuple-element.28), channel_id=1, source_target_pairs={{0,12},{2,14},{4,8},{6,10},{8,4},{10,6},{12,0},{14,2},{1,13},{3,15... | collective-permute-start | bytes 1769480 | tf_op jit(solution)/shard_map/ppermute | solution.py:24
  341.5 102.5 %collective-permute-start.4 = (bf16[1,144,2048]{2,1,0:T(8,128)(2,1)}, bf16[1,144,2048]{2,1,0:T(8,128)(2,1)}, u32[]{:S(2)}, u32[]{:S(2)}) collective-permute-start(bf16[1,144,2048]{2,1,0:T(8,128)(2,1)} %get-tuple-element.29), channel_id=1, source_target_pairs={{0,10},{2,8},{4,14},{6,12},{8,2},{10,0},{12,6},{14,4},{1,11},{3,9}... | collective-permute-start | bytes 1769480 | tf_op jit(solution)/shard_map/ppermute | solution.py:24
  341.6 51.2 %collective-permute-start.1 = (bf16[1,144,2048]{2,1,0:T(8,128)(2,1)}, bf16[1,144,2048]{2,1,0:T(8,128)(2,1)}, u32[]{:S(2)}, u32[]{:S(2)}) collective-permute-start(bf16[1,144,2048]{2,1,0:T(8,128)(2,1)} %get-tuple-element.32), channel_id=1, source_target_pairs={{0,4},{2,6},{4,0},{6,2},{8,12},{10,14},{12,8},{14,10},{1,5},{3,7},... | collective-permute-start | bytes 1769480 | tf_op jit(solution)/shard_map/ppermute | solution.py:24
  352.6 52.9 %collective-permute-start.2 = (bf16[1,144,2048]{2,1,0:T(8,128)(2,1)}, bf16[1,144,2048]{2,1,0:T(8,128)(2,1)S(1)}, u32[]{:S(2)}, u32[]{:S(2)}) collective-permute-start(bf16[1,144,2048]{2,1,0:T(8,128)(2,1)} %get-tuple-element.31), channel_id=1, source_target_pairs={{0,6},{2,4},{4,2},{6,0},{8,14},{10,12},{12,10},{14,8},{1,7},{3,5},... | collective-permute-start | bytes 1769480 | tf_op jit(solution)/shard_map/ppermute | solution.py:24
  392.8 50.2 %collective-permute-start.3 = (bf16[1,144,2048]{2,1,0:T(8,128)(2,1)}, bf16[1,144,2048]{2,1,0:T(8,128)(2,1)S(1)}, u32[]{:S(2)}, u32[]{:S(2)}) collective-permute-start(bf16[1,144,2048]{2,1,0:T(8,128)(2,1)} %get-tuple-element.30), channel_id=1, source_target_pairs={{0,8},{2,10},{4,12},{6,14},{8,0},{10,2},{12,4},{14,6},{1,9},{3,11}... | collective-permute-start | bytes 1769480 | tf_op jit(solution)/shard_map/ppermute | solution.py:24
Sparse Core Ops, SparseCore 0:
  297.5 42.2 reduce-scatter.7
  342.7 43.3 reduce-scatter.5
  388.9 43.3 reduce-scatter.3
